TPU v7x, 512 devices: a whole 4x4x16 slice. The times are simulated.
512 devices in a mesh: dp: 2 (over core), fsdp: 32 (over y, z_lo), tensor: 8 (over z_hi, x).
Axes of the slice: x: 4, y: 4, z: 16 (z_hi: 2, z_lo: 8; z = z_hi * 8 + z_lo), core: 2. Of those that a mesh axis runs over, the one named last changes fastest.
Arguments:
- tokens: bfloat16 [16384, 4096], P(('dp', 'fsdp', 'tensor')), may hold values from -40 to 40
- norm_gain: float32 [4096], replicated, may hold values from 0.5 to 1.5
- tile_values: bfloat16 [512, 128, 128], P(('fsdp', 'tensor')), may hold values from -0.25 to 0.25
- tile_rows: int32 [8, 64], P('tensor'), may hold values from 0 to 31, as said below
- tile_cols: int32 [8, 64], P('tensor'), may hold values from 0 to 13
- tile_counts: int32 [8, 32], P('tensor'), may hold values from 0 to 2, as said below
- grad_out: bfloat16 [16384, 14336], P(('dp', 'fsdp'), 'tensor'), may hold values from -3 to 3
Outputs:
- mixed: bfloat16 [16384, 14336], P(('dp', 'fsdp'), 'tensor')
- grad_x: bfloat16 [16384, 4096], P(('dp', 'fsdp', 'tensor'))
- grad_gain: float32 [4096], replicated
- grad_tiles: float32 [512, 128, 128], P(('fsdp', 'tensor'))
Inputs may be any that keep to these rules, and one draw needn't show every extreme that they name: `tile_counts`: for each tensor index the counts over the 32 fsdp shards sum to 56, and some shard holds exactly 2. `tile_rows`: within one tensor index the (row, column) pairs of held slots are all different.
All inputs are finite; a program needn't handle non-finite values.
Results may differ from a plain program's by a relative error of at most 0.013.
Values may be sent and summed in bfloat16 or wider, within the bound.
A program may use at most 128 MiB of HBM per device.

v0:
```python
import jax
import jax.numpy as jnp
from jax import lax
from jax.sharding import PartitionSpec as P


def tile_forward(group_rows, values, rows_list, cols_list, col_tiles):
    tile_size = values.shape[1]
    blocks = group_rows.reshape(group_rows.shape[0], -1, tile_size)
    picked = jnp.take(blocks, rows_list, axis=1)
    product = jnp.einsum("tsk,skn->tsn", picked, values, preferred_element_type=jnp.float32)
    placed = (
        jnp.zeros((group_rows.shape[0], col_tiles, tile_size), jnp.float32)
        .at[:, cols_list]
        .add(product)
    )
    return placed.reshape(group_rows.shape[0], col_tiles * tile_size)


def tile_backward(grad_rows, values, rows_list, cols_list, row_tiles):
    tile_size = values.shape[1]
    blocks = grad_rows.reshape(grad_rows.shape[0], -1, tile_size)
    picked = jnp.take(blocks, cols_list, axis=1)
    product = jnp.einsum("tsn,skn->tsk", picked, values, preferred_element_type=jnp.float32)
    placed = (
        jnp.zeros((grad_rows.shape[0], row_tiles, tile_size), jnp.float32)
        .at[:, rows_list]
        .add(product)
    )
    return placed.reshape(grad_rows.shape[0], row_tiles * tile_size)


def per_device(tokens, norm_gain, tile_values, tile_rows, tile_cols, tile_counts, grad_out):
    tile_size = tile_values.shape[1]
    slot_cap = tile_values.shape[0]
    row_tiles = tokens.shape[1] // tile_size
    col_tiles = grad_out.shape[1] // tile_size
    rows_list = tile_rows[0]
    cols_list = tile_cols[0]
    shard_counts = tile_counts[0]
    held_all = (jnp.arange(slot_cap)[None, :] < shard_counts[:, None]).reshape(-1)
    own_held = jnp.arange(slot_cap) < shard_counts[lax.axis_index("fsdp")]
    local_float = tokens.astype(jnp.float32)
    inv_rms = lax.rsqrt(jnp.mean(local_float * local_float, axis=1, keepdims=True) + 1e-05)
    scaled = local_float * inv_rms
    normed = (scaled * norm_gain).astype(jnp.bfloat16)
    group_rows = lax.all_gather(normed, "tensor", axis=0, tiled=True)
    gathered = lax.all_gather(tile_values, "fsdp", axis=0, tiled=True)
    kept_values = jnp.where(held_all[:, None, None], gathered, jnp.zeros_like(gathered))
    outputs = tile_forward(group_rows, kept_values, rows_list, cols_list, col_tiles)
    mixed = outputs.astype(jnp.bfloat16)
    input_grad = lax.psum_scatter(
        tile_backward(grad_out, kept_values, rows_list, cols_list, row_tiles).astype(jnp.bfloat16),
        "tensor",
        scatter_dimension=0,
        tiled=True,
    ).astype(jnp.float32)
    x_blocks = group_rows.reshape(group_rows.shape[0], row_tiles, tile_size)
    g_blocks = grad_out.reshape(grad_out.shape[0], col_tiles, tile_size)
    picked_x = jnp.take(x_blocks, rows_list, axis=1)
    picked_g = jnp.take(g_blocks, cols_list, axis=1)
    grad_shard = lax.psum_scatter(
        jnp.einsum("tsk,tsn->skn", picked_x, picked_g, preferred_element_type=jnp.float32),
        "fsdp",
        scatter_dimension=0,
        tiled=True,
    )
    grad_shard = jnp.where(own_held[:, None, None], grad_shard, jnp.zeros_like(grad_shard))
    grad_tiles = lax.psum(grad_shard, "dp")
    gain_part = jnp.sum(input_grad * scaled, axis=0)
    grad_gain = lax.psum(gain_part, ("dp", "fsdp", "tensor"))
    hidden_grad = input_grad * norm_gain
    grad_x = (
        inv_rms * (hidden_grad - scaled * jnp.mean(hidden_grad * scaled, axis=1, keepdims=True))
    ).astype(jnp.bfloat16)
    return (mixed, grad_x, grad_gain, grad_tiles)


def solution(mesh):
    placed = (
        P(("dp", "fsdp", "tensor"), None),
        P(),
        P(("fsdp", "tensor"), None, None),
        P("tensor", None),
        P("tensor", None),
        P("tensor", None),
        P(("dp", "fsdp"), "tensor"),
    )
    return jax.shard_map(
        per_device,
        mesh=mesh,
        in_specs=placed,
        out_specs=(
            P(("dp", "fsdp"), "tensor"),
            P(("dp", "fsdp", "tensor"), None),
            P(),
            P(("fsdp", "tensor"), None, None),
        ),
        check_vma=False,
    )
```

profile of v0, /device:TPU:1, one launch (start us, length us, event | category | flops | bytes accessed | tf_op | source)
XLA Modules:
  0.0 848.3 jit_solution(9026113694259479338)
XLA Ops:
  7.9 1.5 copy.32
  11.6 3.1 gather_fusion.1
  14.7 207.7 %all-gather.3.cloned.1.call-done = bf16[64,128,128]{2,1,0:T(8,128)(2,1)} async-done(((bf16[2,128,128]{2,1,0:T(8,128)(2,1)}), bf16[64,128,128]{2,1,0:T(8,128)(2,1)}) %all-gather.3.cloned.1.call-update) | async-done | bytes 2097168 | tf_op jit(solution)/shard_map/all_gather | solution.py:48
  222.3 7.4 fusion.2
  229.8 2.4 broadcast_in_dim.57
  232.2 19.3 %scatter_fusion.1 = f32[256,32,128]{2,0,1:T(8,128)} fusion(f32[256,32,128]{2,0,1:T(8,128)} %broadcast_in_dim.57, s32[64]{0:T(128)S(1)} %fusion.18, f32[64,256,128]{2,1,0:T(8,128)} %fusion.2), kind=kCustom, calls=%fused_computation.3 | custom fusion | flops 2097152 | bytes 25166080 | tf_op jit(solution)/shard_map/scatter-add | solution.py:28
  251.5 2.5 convert_element_type.28
  254.0 2.9 copy.34
  256.9 4.1 copy.39
  261.3 162.9 %reduce-scatter.7.cloned.1.call-done = bf16[32,4096]{1,0:T(8,128)(2,1)} async-done(((bf16[256,4096]{1,0:T(8,128)(2,1)}), bf16[32,4096]{1,0:T(8,128)(2,1)}) %reduce-scatter.7.cloned.1.call-update) | async-done | bytes 262160 | tf_op jit(solution)/shard_map/reduce_scatter | solution.py:52
  425.5 1.9 fusion.12
  427.5 109.9 %all-gather.5.cloned.1.call-done = bf16[256,4096]{1,0:T(8,128)(2,1)} async-done(((bf16[32,4096]{1,0:T(8,128)(2,1)}), bf16[256,4096]{1,0:T(8,128)(2,1)}) %all-gather.5.cloned.1.call-update) | async-done | bytes 2097168 | tf_op jit(solution)/shard_map/all_gather | solution.py:47
  537.4 4.1 copy.29
  541.5 3.2 copy.30
  544.7 3.0 gather_fusion
  547.7 7.0 fusion
  556.6 102.9 %psum.14 = f32[4096]{0:T(1024)} all-reduce(f32[4096]{0:T(1024)S(1)} %get-tuple-element.18), channel_id=1, replica_groups=mesh['dp'=2,'fsdp'=32,'tensor'=8] {'dp','fsdp','tensor'}, use_global_device_ids=true, to_apply=%region_6.9 | all-reduce | flops 4096 | bytes 32768 | tf_op jit(solution)/shard_map/psum | solution.py:71
  659.5 120.1 %reduce-scatter.5.cloned.1.call-done = f32[2,128,128]{2,1,0:T(8,128)} async-done(((f32[64,128,128]{2,1,0:T(8,128)}), f32[2,128,128]{2,1,0:T(8,128)}) %reduce-scatter.5.cloned.1.call-update) | async-done | bytes 131088 | tf_op jit(solution)/shard_map/reduce_scatter | solution.py:62
  779.7 1.6 broadcast_select_fusion.9
  781.3 6.7 fusion.5
  788.2 12.4 %scatter_fusion = f32[256,14,128]{2,0,1:T(8,128)S(1)} fusion(f32[256,14,128]{2,0,1:T(8,128)S(1)} %broadcast_in_dim.54, s32[64]{0:T(128)S(1)} %fusion.17, f32[64,256,128]{2,1,0:T(8,128)} %fusion.5), kind=kCustom, calls=%fused_computation.2 | custom fusion | flops 2097152 | bytes 25166080 | tf_op jit(solution)/shard_map/scatter-add | solution.py:15
  801.4 1.4 copy.37
  802.7 37.5 %all-reduce.2.cloned.1.call-done = f32[2,128,128]{2,1,0:T(8,128)} async-done(((f32[2,128,128]{2,1,0:T(8,128)}), f32[2,128,128]{2,1,0:T(8,128)}) %all-reduce.2.cloned.1.call-update) | async-done | bytes 131088 | tf_op jit(solution)/shard_map/psum | solution.py:69
  840.2 1.6 copy.44
  (41 shorter events, 7.2 us)
Async XLA Ops:
  7.2 215.2 %all-gather.3.cloned.1.call-start = ((), (), s32[]{:S(2)}) async-start(), calls=%async_computation.2 | async-start | bytes 2162688 | tf_op jit(solution)/shard_map/all_gather | solution.py:48
  7.9 416.3 %reduce-scatter.7.cloned.1.call-start = ((), (), s32[]{:S(2)}) async-start(), calls=%async_computation.6 | async-start | bytes 2359296 | tf_op jit(solution)/shard_map/reduce_scatter | solution.py:52
  11.6 3.1 copy-start.4
  11.6 3.1 copy-start.5
  256.9 4.2 copy-start.1
  256.9 167.3 %copy-start.2 = (f32[4096]{0:T(1024)S(1)}, f32[4096]{0:T(1024)}, u32[]{:S(2)}) copy-start(f32[4096]{0:T(1024)} %param.12) | copy-start | bytes 49156
  261.1 276.3 %all-gather.5.cloned.1.call-start = ((), (), s32[]{:S(2)}) async-start(), calls=%async_computation.3 | async-start | bytes 2359296 | tf_op jit(solution)/shard_map/all_gather | solution.py:47
  427.4 352.2 %reduce-scatter.5.cloned.1.call-start = ((), (), s32[]{:S(2)}) async-start(), calls=%async_computation.4 | async-start | bytes 4325376 | tf_op jit(solution)/shard_map/reduce_scatter | solution.py:62
  554.7 0.7 copy-start.3
  554.7 226.6 %copy-start = (bf16[64,128,128]{2,1,0:T(8,128)(2,1)S(1)}, bf16[64,128,128]{2,1,0:T(8,128)(2,1)}, u32[]{:S(2)}) copy-start(bf16[64,128,128]{2,1,0:T(8,128)(2,1)} %all-gather.3.cloned.1.call-done) | copy-start | bytes 6291460
  554.7 285.5 %all-reduce.2.cloned.1.call-start = ((), (), s32[]{:S(2)}) async-start(), calls=%async_computation.5 | async-start | bytes 262144 | tf_op jit(solution)/shard_map/psum | solution.py:69
Sparse Core Ops, SparseCore 0:
  10.1 212.2 all-gather.2
  261.2 162.9 reduce-scatter.6
  428.4 108.8 all-gather.4
  554.9 224.7 reduce-scatter.4
  783.2 56.9 all-reduce.1
where the time goes:
time: 849 us; the launch traced here: 848 us
  waiting for transfers between devices  639 us (75%)
  blocking collectives  103 us (12%)
  other arithmetic  41.4 us (5%)
  local copies, waits for them, and re-layouts  29.9 us (4%)
  matrix products  21.2 us (2%)
  between operations  13.9 us (2%)
    all_gather x1, waiting for transfers between devices, per_device(): gathered = lax.all_gather(tile_values, 'fsdp', axis=0, tiled=True)  208 us
    reduce_scatter x1, waiting for transfers between devices, per_device(): lax.psum_scatter(tile_backward(grad_out, kept_values, rows_list, cols_lis...  163 us
    reduce_scatter x1, waiting for transfers between devices, per_device(): lax.psum_scatter(jnp.einsum('tsk,tsn->skn', picked_x, picked_g, preferred...  120 us
    all_gather x1, waiting for transfers between devices, per_device(): group_rows = lax.all_gather(normed, 'tensor', axis=0, tiled=True)  110 us
    psum x1, blocking collectives, per_device(): grad_gain = lax.psum(gain_part, ('dp', 'fsdp', 'tensor'))  103 us
    psum x1, waiting for transfers between devices, per_device(): grad_tiles = lax.psum(grad_shard, 'dp')  37.5 us
    scatter-add x1, other arithmetic, tile_backward(): placed = jnp.zeros((grad_rows.shape[0], row_tiles, tile_size), jnp.float3...  19.3 us
  transfers between devices with their start and end apart: 5, of which 5 were waited for; matrix products, arithmetic and copies ran while one was open for 3% of the time, Pallas kernels for 0%

commit v1 on v0

v1 whole, which is shorter than its diff:
```python
import functools

import jax
import jax.numpy as jnp
from jax import lax
from jax.experimental import pallas as pl
from jax.experimental.pallas import tpu as pltpu
from jax.sharding import PartitionSpec as P

MESH = pl.DeviceIdType.MESH
F32 = jnp.float32
BF16 = jnp.bfloat16
RT = 32
CT = 14
SLOTS = 64
NSEM = 128


class Net:
    def __init__(self, ssem, rsem, anyone):
        self.ssem, self.rsem, self.anyone = ssem, rsem, anyone
        self.sent = []

    def send(self, src, dst, device):
        i = len(self.sent)
        copy = pltpu.make_async_remote_copy(
            src_ref=src,
            dst_ref=dst,
            send_sem=self.ssem.at[i],
            recv_sem=self.rsem.at[i],
            device_id=device,
            device_id_type=MESH,
        )
        copy.start()
        self.sent.append(copy)
        return i

    def recv(self, i, ref):
        pltpu.make_async_remote_copy(
            src_ref=ref,
            dst_ref=ref,
            send_sem=self.ssem.at[i],
            recv_sem=self.rsem.at[i],
            device_id=self.anyone,
            device_id_type=MESH,
        ).wait_recv()


def lanes(i):
    return pl.ds(pl.multiple_of(i * 128, 128), 128)


def slot_tables(rows, cols, counts, zl, table):
    sub = lax.broadcasted_iota(jnp.int32, (SLOTS, SLOTS), 0)
    lane = lax.broadcasted_iota(jnp.int32, (SLOTS, SLOTS), 1)
    wide = lax.broadcasted_iota(jnp.int32, (SLOTS, 128), 1)
    slot = lax.broadcasted_iota(jnp.int32, (SLOTS, 1), 0)

    def over_lanes(mask, value):
        return jnp.sum(jnp.where(mask, value, 0), axis=1, keepdims=True)

    def over_slots(mask, value):
        return jnp.sum(jnp.where(mask, value, 0), axis=0, keepdims=True)

    def row(column_vector):
        return over_slots(sub == lane, column_vector)

    def put(k, vector):
        table[pl.ds(k, 1), :] = vector

    table[...] = jnp.zeros_like(table)
    row_of, col_of = over_lanes(sub == lane, rows), over_lanes(sub == lane, cols)
    shard = lax.broadcasted_iota(jnp.int32, (SLOTS, 32), 0) >> 1
    shard_lane = lax.broadcasted_iota(jnp.int32, (SLOTS, 32), 1)
    count = over_lanes(shard == shard_lane, counts)
    j = slot & 1
    held = count > j
    apart = ((slot >> 1) & 7) ^ zl
    place = ((apart & 1) << 2) | (apart & 2) | (apart >> 2)
    stored = j * 32 + (slot >> 4) * 8 + place
    for base, key, other in ((0, row_of, col_of), (5, col_of, row_of)):
        key = jnp.where(held, key, 64)
        order = key * 64 + slot
        rank = over_lanes(row(order) < order, 1)
        same = over_lanes((row(key) == key) & (lane < sub), 1)
        at = rank == wide
        for k, vector in ((0, stored), (1, other), (2, jnp.minimum(same, 1))):
            put(base + k, over_slots(at, vector))
        put(base + 3, jnp.maximum(over_slots(key <= wide, 1) - 1, 0))
        put(base + 4, jnp.minimum(over_slots(key == wide, 1), 1))
    at = stored == wide
    put(10, over_slots(at, row_of))
    put(11, over_slots(at, col_of))


def kernel(
    tok_hbm, gain, tv_hbm, rows, cols, counts, counts_s, go_hbm,
    mixed_hbm, gx_hbm, gg_hbm, gt_hbm,
    tok, go, gs, gt, x_all, scaled, inv, w, pb, pf, s, r, zs, zr, ig,
    dt, dr, e, es, yr, fs, fa, fr, tiles, mx, ox, table, sm,
    gp, gc, g1, gx4, gy, gh, gz, ga, ssem, rsem, lsem,
):
    d, f, t = lax.axis_index("dp"), lax.axis_index("fsdp"), lax.axis_index("tensor")
    h, x, y, zl = t // 4, lax.rem(t, 4), f // 8, lax.rem(f, 8)
    core = {"dp": 1 - d}
    other_half = {"tensor": lax.rem(t + 4, 8)}
    oc = lax.rem(t + 4, 8)

    def x_peer(k):
        return {"tensor": h * 4 + lax.rem(x + k, 4)}

    def y_peer(k):
        return {"fsdp": lax.rem(y + k, 4) * 8 + zl}

    z4 = {"fsdp": y * 8 + lax.rem(zl + 4, 8)}
    z2 = {"fsdp": f + 2 - 4 * lax.rem(zl // 2, 2)}
    z1 = {"fsdp": f + 1 - 2 * lax.rem(zl, 2)}
    partners = [core, other_half, z4, z2, z1]
    partners += [x_peer(k) for k in (1, 2, 3)] + [y_peer(k) for k in (1, 2, 3)]

    own_w = d * 32 + y * 8

    loads = [
        pltpu.make_async_copy(tok_hbm, tok, lsem.at[0]),
        pltpu.make_async_copy(tv_hbm.at[0], w.at[y * 8], lsem.at[1]),
        pltpu.make_async_copy(tv_hbm.at[1], w.at[32 + y * 8], lsem.at[2]),
        pltpu.make_async_copy(go_hbm, go, lsem.at[3]),
    ]
    for c in loads:
        c.start()
    barrier = pltpu.get_barrier_semaphore()
    for p in partners:
        pl.semaphore_signal(barrier, inc=1, device_id=p, device_id_type=MESH)

    loads[0].wait()

    def square(i, a):
        for u in range(4):
            v = tok[:, lanes(i * 4 + u)].astype(F32)
            a = a + v * v
        return a

    total = lax.fori_loop(0, RT // 4, square, jnp.zeros((32, 128), F32))
    inv_rms = lax.rsqrt(jnp.sum(total, axis=1, keepdims=True) * (1.0 / 4096.0) + 1e-05)
    inv[...] = jnp.broadcast_to(inv_rms, (32, 128))

    def norm(i, _):
        for u in range(4):
            rt = i * 4 + u
            v = tok[:, lanes(rt)].astype(F32) * inv[...]
            scaled[rt] = v
            x_all[t, rt] = (v * gain[pl.ds(rt, 1), :]).astype(BF16)
        return 0

    lax.fori_loop(0, RT // 4, norm, 0)
    loads[1].wait()
    loads[2].wait()
    pl.semaphore_wait(barrier, len(partners))

    net = Net(ssem, rsem, core)

    def w_at(base, lo, n):
        return w.at[pl.ds(base + lo, n)]

    def w_to_y(lo, n):
        return [net.send(w_at(own_w, lo, n), w_at(own_w, lo, n), y_peer(k)) for k in (1, 2, 3)]

    def x_chunk(c, q):
        return x_all.at[c, pl.ds(q * 8, 8)]

    wz = [net.send(w_at(own_w, 0, 1), w_at(own_w, 1, 1), z4)]
    wy = [w_to_y(0, 1)]
    xz = [net.send(x_chunk(t, 0), x_chunk(t, 0), other_half)]
    xown = [net.send(x_all.at[t], x_all.at[t], x_peer(k)) for k in (1, 2, 3)]
    xz.append(net.send(x_chunk(t, 1), x_chunk(t, 1), other_half))

    slot_tables(rows[...], cols[...], counts[...], zl, table)
    to_smem = pltpu.make_async_copy(table, sm, lsem.at[4])
    to_smem.start()

    net.recv(wz[0], w_at(own_w, 1, 1))
    wz.append(net.send(w_at(own_w, 0, 2), w_at(own_w, 2, 2), z2))
    wy.append(w_to_y(1, 1))

    loads[3].wait()
    for c in range(CT):
        v = go[:, c * 128 : (c + 1) * 128]
        gs[c] = v
        gt[c] = v.T

    net.recv(wz[1], w_at(own_w, 2, 2))
    wz.append(net.send(w_at(own_w, 0, 4), w_at(own_w, 4, 4), z1))
    wy.append(w_to_y(2, 2))
    xz.append(net.send(x_chunk(t, 2), x_chunk(t, 2), other_half))
    xz.append(net.send(x_chunk(t, 3), x_chunk(t, 3), other_half))

    xfwd = []

    def forward(q):
        net.recv(xz[q], x_chunk(oc, q))
        xfwd.append([net.send(x_chunk(oc, q), x_chunk(oc, q), x_peer(k)) for k in (1, 2, 3)])

    net.recv(wz[2], w_at(own_w, 4, 4))
    wy.append(w_to_y(4, 4))
    wc = [net.send(w_at(own_w, 1, 7), w_at(own_w, 1, 7), core)]
    forward(0)
    for k in (1, 2, 3):
        base = d * 32 + lax.rem(y + 4 - k, 4) * 8
        for ids, (lo, n) in zip(wy, ((0, 1), (1, 1), (2, 2), (4, 4))):
            net.recv(ids[k - 1], w_at(base, lo, n))
        wc.append(net.send(w_at(base, 0, 8), w_at(base, 0, 8), core))
    forward(1)
    other_w = (1 - d) * 32
    net.recv(wc[0], w_at(other_w + y * 8, 1, 7))
    for k in (1, 2, 3):
        net.recv(wc[k], w_at(other_w + lax.rem(y + 4 - k, 4) * 8, 0, 8))
    to_smem.wait()

    def back(b, acc):
        for u in range(4):
            i = b * 4 + u
            prod = lax.dot_general(gs[sm[1, i]], w[sm[0, i]], (((1,), (1,)), ((), ())), preferred_element_type=F32)
            acc = acc * sm[2, i].astype(F32) + prod
            pb[i] = acc.astype(BF16)
        return acc

    lax.fori_loop(0, SLOTS // 4, back, jnp.zeros((256, 128), F32))
    rs_other, rs_own = [], []

    def assemble(q):
        def one(rt, _):
            v = pb[sm[3, rt]].astype(F32) * sm[4, rt].astype(F32)
            s[:, rt] = v.astype(BF16).reshape(8, 32, 128)
            return 0

        lax.fori_loop(q * 8, q * 8 + 8, one, 0)

    def scatter(half, slot, q):
        ids = []
        for k in (1, 2, 3):
            to = half * 4 + lax.rem(x + k, 4)
            ids.append(net.send(s.at[to, pl.ds(q * 8, 8)], r.at[slot, k - 1, pl.ds(q * 8, 8)], x_peer(k)))
        return ids

    for q in range(4):
        assemble(q)
        rs_other.append(scatter(1 - h, 0, q))
    forward(2)
    for q in range(4):
        rs_own.append(scatter(h, 1, q))
    forward(3)

    zids = []

    def reduce_other(q):
        for k in (1, 2, 3):
            net.recv(rs_other[q][k - 1], r.at[0, k - 1, pl.ds(q * 8, 8)])

        def one(rt, _):
            v = s[oc, rt].astype(F32) + r[0, 0, rt].astype(F32)
            v = v + r[0, 1, rt].astype(F32) + r[0, 2, rt].astype(F32)
            zs[rt] = v.astype(BF16)
            return 0

        lax.fori_loop(q * 8, q * 8 + 8, one, 0)
        part = pl.ds(q * 8, 8)
        zids.append(net.send(zs.at[part], zr.at[part], other_half))

    for k in (1, 2, 3):
        net.recv(xown[k - 1], x_all.at[h * 4 + lax.rem(x + 4 - k, 4)])
    reduce_other(0)
    reduce_other(1)
    for k in (1, 2, 3):
        for q in range(4):
            net.recv(xfwd[q][k - 1], x_chunk((1 - h) * 4 + lax.rem(x + 4 - k, 4), q))

    def tile_grad(j, yy, out, cast):
        def one(q, _):
            p = j * 32 + yy * 8 + q
            xs = x_all[:, sm[10, p]].reshape(256, 128)
            out[yy * 8 + q] = jnp.dot(gt[sm[11, p]], xs, preferred_element_type=F32).astype(cast)
            return 0

        lax.fori_loop(0, 8, one, 0, unroll=True)

    def tiles8(ref, yy):
        return ref.at[pl.ds(yy * 8, 8)]

    dc = {}
    for k in (1, 2, 3, 0):
        yy = lax.rem(y + k, 4)
        tile_grad(1 - d, yy, dt, BF16)
        dc[k] = net.send(tiles8(dt, yy), tiles8(dr, yy), core)
    reduce_other(2)
    reduce_other(3)
    ty = {}
    for k in (1, 2, 3, 0):
        yy = lax.rem(y + k, 4)
        tile_grad(d, yy, e, F32)
        net.recv(dc[k], tiles8(dr, yy))

        def join(q, _):
            i = yy * 8 + q
            v = e[i] + dr[i].astype(F32)
            if k:
                es[i] = v.astype(BF16)
            else:
                e[i] = v
            return 0

        lax.fori_loop(0, 8, join, 0)
        if k:
            ty[k] = net.send(tiles8(es, yy), yr.at[k - 1], y_peer(k))

    def gain_part(rt, _):
        v = s[:, rt].astype(F32) * x_all[:, rt].astype(F32)
        gp[rt] = jnp.sum(v.reshape(256, 128), axis=0, keepdims=True)
        return 0

    lax.fori_loop(0, RT, gain_part, 0)
    gid = net.send(gp.at[pl.ds((1 - d) * 16, 16)], gc, core)

    def ahead(b, acc):
        for u in range(4):
            i = b * 4 + u
            xs = x_all[:, sm[6, i]].reshape(256, 128)
            prod = jnp.dot(xs, w[sm[5, i]], preferred_element_type=F32)
            acc = acc * sm[7, i].astype(F32) + prod
            pf[i] = acc.astype(BF16)
        return acc

    lax.fori_loop(0, SLOTS // 4, ahead, jnp.zeros((256, 128), F32))
    for c in range(CT):
        v = pf[sm[8, c]].astype(F32) * sm[9, c].astype(F32)
        mx[:, c * 128 : (c + 1) * 128] = v.astype(BF16)
    mixed_out = pltpu.make_async_copy(mx, mixed_hbm, lsem.at[5])
    mixed_out.start()

    net.recv(gid, gc)
    for i in range(16):
        g1[i] = gp[d * 16 + i] + gc[i]
    gids = [net.send(g1.at[pl.ds(lax.rem(x + k, 4) * 4, 4)], gx4.at[k - 1], x_peer(k)) for k in (1, 2, 3)]

    for k in (1, 2, 3):
        for q in range(4):
            net.recv(rs_own[q][k - 1], r.at[1, k - 1, pl.ds(q * 8, 8)])

    def own(rt, _):
        v = s[t, rt].astype(F32) + r[1, 0, rt].astype(F32)
        ig[rt] = v + r[1, 1, rt].astype(F32) + r[1, 2, rt].astype(F32)
        return 0

    lax.fori_loop(0, RT, own, 0)

    for k in (1, 2, 3):
        net.recv(gids[k - 1], gx4.at[k - 1])
    for i in range(4):
        gy[y, i] = g1[x * 4 + i] + gx4[0, i] + gx4[1, i] + gx4[2, i]
    gids = [net.send(gy.at[y], gy.at[y], y_peer(k)) for k in (1, 2, 3)]

    for k in (1, 2, 3):
        net.recv(ty[k], yr.at[k - 1])

    def sum_y(q):
        v = e[y * 8 + q] + yr[0, q].astype(F32)
        return v + yr[1, q].astype(F32) + yr[2, q].astype(F32)

    for q in range(4, 8):
        fs[q] = sum_y(q).astype(BF16)
    tz1 = net.send(fs.at[pl.ds(4, 4)], fr.at[pl.ds(4, 4)], z1)
    for q in range(4):
        fa[q] = sum_y(q)

    for k in (1, 2, 3):
        net.recv(gids[k - 1], gy.at[lax.rem(y + 4 - k, 4)])
    for i in range(4):
        gh[0, i] = gy[0, i] + gy[1, i] + gy[2, i] + gy[3, i]
    gid = net.send(gh.at[0], gh.at[1], other_half)

    net.recv(tz1, fr.at[pl.ds(4, 4)])
    for q in (2, 3):
        fs[q] = (fa[q] + fr[q + 4].astype(F32)).astype(BF16)
    tz2 = net.send(fs.at[pl.ds(2, 2)], fr.at[pl.ds(2, 2)], z2)
    for q in (0, 1):
        fa[q] = fa[q] + fr[q + 4].astype(F32)

    net.recv(gid, gh.at[1])
    for i in range(4):
        gz[0, i] = gh[0, i] + gh[1, i]
    gid = net.send(gz.at[0], gz.at[1], z4)

    net.recv(tz2, fr.at[pl.ds(2, 2)])
    fs[1] = (fa[1] + fr[3].astype(F32)).astype(BF16)
    tz3 = net.send(fs.at[pl.ds(1, 1)], fr.at[pl.ds(1, 1)], z4)
    fa[0] = fa[0] + fr[2].astype(F32)

    net.recv(gid, gz.at[1])
    for i in range(4):
        gz[2, i] = gz[0, i] + gz[1, i]
    gid = net.send(gz.at[2], gz.at[3], z2)

    def hidden(rt, a):
        v = (ig[rt] + zr[rt].astype(F32)) * gain[pl.ds(rt, 1), :]
        ig[rt] = v
        return a + v * scaled[rt]

    acc = jnp.zeros((32, 128), F32)
    for q in range(2):
        net.recv(zids[q], zr.at[pl.ds(q * 8, 8)])
        acc = lax.fori_loop(q * 8, q * 8 + 8, hidden, acc)

    net.recv(gid, gz.at[3])
    for i in range(4):
        gz[4, i] = gz[2, i] + gz[3, i]
    gid = net.send(gz.at[4], gz.at[5], z1)

    net.recv(tz3, fr.at[pl.ds(1, 1)])
    keep = jnp.where(counts_s[0, f] > d, 1.0, 0.0)
    tiles[d] = (fa[0] + fr[1].astype(F32)).T * keep
    tc = net.send(tiles.at[d], tiles.at[d], core)

    for q in range(2, 4):
        net.recv(zids[q], zr.at[pl.ds(q * 8, 8)])
        acc = lax.fori_loop(q * 8, q * 8 + 8, hidden, acc)

    net.recv(gid, gz.at[5])
    mine = d * 16 + x * 4
    for i in range(4):
        ga[mine + i] = (gz[4, i] + gz[5, i]) / gain[pl.ds(mine + i, 1), :]
    gids = [net.send(ga.at[pl.ds(mine, 4)], ga.at[pl.ds(mine, 4)], x_peer(k)) for k in (1, 2, 3)]

    mean = jnp.sum(acc, axis=1, keepdims=True) * (1.0 / 4096.0)

    def finish(i, _):
        for u in range(4):
            rt = i * 4 + u
            v = inv[...] * (ig[rt] - scaled[rt] * mean)
            ox[:, lanes(rt)] = v.astype(BF16)
        return 0

    lax.fori_loop(0, RT // 4, finish, 0)
    gx_out = pltpu.make_async_copy(ox, gx_hbm, lsem.at[6])
    gx_out.start()

    for k in (1, 2, 3):
        net.recv(gids[k - 1], ga.at[pl.ds(d * 16 + lax.rem(x + 4 - k, 4) * 4, 4)])
    gid = net.send(ga.at[pl.ds(d * 16, 16)], ga.at[pl.ds(d * 16, 16)], core)
    net.recv(tc, tiles.at[1 - d])
    gt_out = pltpu.make_async_copy(tiles, gt_hbm, lsem.at[7])
    gt_out.start()
    net.recv(gid, ga.at[pl.ds((1 - d) * 16, 16)])
    gg_out = pltpu.make_async_copy(ga, gg_hbm, lsem.at[8])
    gg_out.start()
    for copy in net.sent:
        copy.wait_send()
    for copy in (mixed_out, gx_out, gt_out, gg_out):
        copy.wait()


def per_device(tokens, norm_gain, tile_values, tile_rows, tile_cols, tile_counts, grad_out):
    hbm = pl.BlockSpec(memory_space=pl.ANY)
    vmem = pl.BlockSpec(memory_space=pltpu.VMEM)
    smem = pl.BlockSpec(memory_space=pltpu.SMEM)
    rows8 = (8, RT, 32, 128)
    local = (RT, 32, 128)
    tiles32 = (32, 128, 128)
    mixed, grad_x, grad_gain, grad_tiles = pl.pallas_call(
        kernel,
        out_shape=(
            jax.ShapeDtypeStruct((256, 1792), BF16),
            jax.ShapeDtypeStruct((32, 4096), BF16),
            jax.ShapeDtypeStruct((RT, 1, 128), F32),
            jax.ShapeDtypeStruct((2, 128, 128), F32),
        ),
        in_specs=[hbm, vmem, hbm, vmem, vmem, vmem, smem, hbm],
        out_specs=(hbm, hbm, hbm, hbm),
        scratch_shapes=[
            pltpu.VMEM((32, 4096), BF16),
            pltpu.VMEM((256, 1792), BF16),
            pltpu.VMEM((CT, 256, 128), BF16),
            pltpu.VMEM((CT, 128, 256), BF16),
            pltpu.VMEM(rows8, BF16),
            pltpu.VMEM(local, F32),
            pltpu.VMEM((32, 128), F32),
            pltpu.VMEM((SLOTS, 128, 128), BF16),
            pltpu.VMEM((SLOTS, 256, 128), BF16),
            pltpu.VMEM((SLOTS, 256, 128), BF16),
            pltpu.VMEM(rows8, BF16),
            pltpu.VMEM((2, 3) + local, BF16),
            pltpu.VMEM(local, BF16),
            pltpu.VMEM(local, BF16),
            pltpu.VMEM(local, F32),
            pltpu.VMEM(tiles32, BF16),
            pltpu.VMEM(tiles32, BF16),
            pltpu.VMEM(tiles32, F32),
            pltpu.VMEM(tiles32, BF16),
            pltpu.VMEM((3, 8, 128, 128), BF16),
            pltpu.VMEM((8, 128, 128), BF16),
            pltpu.VMEM((4, 128, 128), F32),
            pltpu.VMEM((8, 128, 128), BF16),
            pltpu.VMEM((2, 128, 128), F32),
            pltpu.VMEM((256, 1792), BF16),
            pltpu.VMEM((32, 4096), BF16),
            pltpu.VMEM((16, 128), jnp.int32),
            pltpu.SMEM((16, 128), jnp.int32),
            pltpu.VMEM((RT, 1, 128), F32),
            pltpu.VMEM((16, 1, 128), F32),
            pltpu.VMEM((16, 1, 128), F32),
            pltpu.VMEM((3, 4, 1, 128), F32),
            pltpu.VMEM((4, 4, 1, 128), F32),
            pltpu.VMEM((2, 4, 1, 128), F32),
            pltpu.VMEM((6, 4, 1, 128), F32),
            pltpu.VMEM((RT, 1, 128), F32),
            pltpu.SemaphoreType.DMA((NSEM,)),
            pltpu.SemaphoreType.DMA((NSEM,)),
            pltpu.SemaphoreType.DMA((9,)),
        ],
        compiler_params=pltpu.CompilerParams(
            collective_id=0, has_side_effects=True, vmem_limit_bytes=52 * 1024 * 1024
        ),
        name="sparse_mlp",
    )(
        tokens, norm_gain.reshape(RT, 128), tile_values, tile_rows, tile_cols, tile_counts,
        tile_counts, grad_out,
    )
    return mixed, grad_x, grad_gain.reshape(4096), grad_tiles


def solution(mesh):
    placed = (
        P(("dp", "fsdp", "tensor"), None),
        P(),
        P(("fsdp", "tensor"), None, None),
        P("tensor", None),
        P("tensor", None),
        P("tensor", None),
        P(("dp", "fsdp"), "tensor"),
    )
    return jax.shard_map(
        per_device,
        mesh=mesh,
        in_specs=placed,
        out_specs=(
            P(("dp", "fsdp"), "tensor"),
            P(("dp", "fsdp", "tensor"), None),
            P(),
            P(("fsdp", "tensor"), None, None),
        ),
        check_vma=False,
    )
```

time: 849 us -> 138 us (0.16)
  waiting for transfers between devices: 639 us -> 0 us
  Pallas kernels: 0 us -> 131 us
  blocking collectives: 103 us -> 0 us
  other arithmetic: 41.4 us -> 0 us
  local copies, waits for them, and re-layouts: 29.9 us -> 6.06 us
  matrix products: 21.2 us -> 0 us
  between operations: 13.9 us -> 0.67 us
    all_gather x2 -> x0, waiting for transfers between devices: 318 us -> none  [the longest x1 208 us: per_device(): gathered = lax.all_gather(tile_values, 'fsdp', axis=0, tiled=True)]
    reduce_scatter x2 -> x0, waiting for transfers between devices: 283 us -> none  [the longest x1 163 us: per_device(): lax.psum_scatter(tile_backward(grad_out, kept_values, rows_list, cols_lis...]
    pallas_call x0 -> x1, Pallas kernels: none -> 131 us  [per_device(): pl.pallas_call(kernel, out_shape=(jax.ShapeDtypeStruct((256, 1792), BF16)...]
    psum x1 -> x0, blocking collectives: 103 us -> none  [per_device(): grad_gain = lax.psum(gain_part, ('dp', 'fsdp', 'tensor'))]
    psum x1 -> x0, waiting for transfers between devices: 37.5 us -> none  [per_device(): grad_tiles = lax.psum(grad_shard, 'dp')]
    scatter-add x2 -> x0, other arithmetic: 31.7 us -> none  [the longest x1 19.3 us: tile_backward(): placed = jnp.zeros((grad_rows.shape[0], row_tiles, tile_size), jnp.float3...]
    dot_general x3 -> x0, matrix products: 21.2 us -> none  [the longest x1 7.42 us: tile_backward(): jnp.einsum('tsn,skn->tsk', picked, values, preferred_element_type=jnp.flo...]
  transfers between devices with their start and end apart: 5 -> 0, of which waited for: 5 -> 0; matrix products, arithmetic and copies ran while one was open for 3% -> 0% of each run, Pallas kernels for 0% -> 0%
where the time goes in v1:
time: 138 us
  Pallas kernels  131 us (95%)
  local copies, waits for them, and re-layouts  6.06 us (4%)
    pallas_call x1, Pallas kernels, per_device(): pl.pallas_call(kernel, out_shape=(jax.ShapeDtypeStruct((256, 1792), BF16)...  131 us
    unnamed x16, local copies, waits for them, and re-layouts  6.06 us

profile of v1, /device:TPU:1, one launch (start us, length us, event | category | flops | bytes accessed | tf_op | source)
XLA Modules:
  0.0 137.8 jit_solution(12815926080927459359)
XLA Ops:
  0.6 0.0 copy-start.3
  0.6 0.0 copy-start.5
  0.7 0.0 copy-start.4
  0.7 0.6 copy-done.3
  1.3 0.0 copy-done.5
  1.3 0.0 copy-done.4
  1.3 0.0 copy-start
  1.3 0.9 copy-done
  2.3 0.0 copy-start.1
  2.3 0.8 copy-done.1
  3.1 0.0 copy-start.2
  3.1 0.7 copy-done.2
  3.8 131.1 %sparse_mlp.1 = (bf16[256,1792]{1,0:T(8,128)(2,1)S(1)}, bf16[32,4096]{1,0:T(8,128)(2,1)S(1)}, f32[32,1,128]{2,1,0:T(1,128)S(1)}, f32[2,128,128]{2,1,0:T(8,128)S(1)}) custom-call(bf16[32,4096]{1,0:T(8,128)(2,1)S(1)} %copy-done, f32[32,128]{1,0:T(8,128)S(1)} %bitcast.2, bf16[2,128,128]{2,1,0:T(8,128)(2,1)S(1)} %copy-done.1, s32[1,64]{1,0:T(1,128)S(1)} %copy-done.4, ...), custom_call_target="tpu_custom_call" | custom-call | tf_op jit(solution)/shard_map/sparse_mlp/pallas_call | solution.py:467
  134.9 0.9 copy.15
  135.9 0.7 copy.16
  136.6 0.6 copy.17
  137.2 0.7 copy.18
Async XLA Ops:
  0.6 0.7 copy-start.3
  0.6 0.7 copy-start.5
  0.7 0.7 copy-start.4
  1.3 0.9 copy-start
  2.3 0.8 copy-start.1
  3.1 0.7 copy-start.2

commit v2 on v1

--- a/solution.py
+++ b/solution.py
@@ -13,7 +13,8 @@
 RT = 32
 CT = 14
 SLOTS = 64
-NSEM = 128
+NSEM = 160
+X_OVER = (0, 2, 3, 3)
 
 
 class Net:
@@ -98,27 +99,35 @@
     mixed_hbm, gx_hbm, gg_hbm, gt_hbm,
     tok, go, gs, gt, x_all, scaled, inv, w, pb, pf, s, r, zs, zr, ig,
     dt, dr, e, es, yr, fs, fa, fr, tiles, mx, ox, table, sm,
-    gp, gc, g1, gx4, gy, gh, gz, ga, ssem, rsem, lsem,
+    gp, gc, gy, gz, ga, ssem, rsem, lsem,
 ):
     d, f, t = lax.axis_index("dp"), lax.axis_index("fsdp"), lax.axis_index("tensor")
     h, x, y, zl = t // 4, lax.rem(t, 4), f // 8, lax.rem(f, 8)
+    z = h * 8 + zl
     core = {"dp": 1 - d}
-    other_half = {"tensor": lax.rem(t + 4, 8)}
     oc = lax.rem(t + 4, 8)
-
-    def x_peer(k):
-        return {"tensor": h * 4 + lax.rem(x + k, 4)}
+    other_half = {"tensor": oc}
+
+    def x_peer(k, dd=0):
+        peer = {"tensor": h * 4 + lax.rem(x + k, 4)}
+        return {**peer, "dp": 1 - d} if dd else peer
 
     def y_peer(k):
         return {"fsdp": lax.rem(y + k, 4) * 8 + zl}
+
+    def z_peer(k):
+        to = lax.rem(z + k, 16)
+        return {"fsdp": y * 8 + lax.rem(to, 8), "tensor": (to // 8) * 4 + x}
 
     z4 = {"fsdp": y * 8 + lax.rem(zl + 4, 8)}
     z2 = {"fsdp": f + 2 - 4 * lax.rem(zl // 2, 2)}
     z1 = {"fsdp": f + 1 - 2 * lax.rem(zl, 2)}
-    partners = [core, other_half, z4, z2, z1]
-    partners += [x_peer(k) for k in (1, 2, 3)] + [y_peer(k) for k in (1, 2, 3)]
+    plane = [(dd, k) for dd in (0, 1) for k in range(4) if dd or k]
+    partners = [x_peer(k, dd) for dd, k in plane]
+    partners += [y_peer(k) for k in (1, 2, 3)] + [z_peer(k) for k in range(1, 16)]
 
     own_w = d * 32 + y * 8
+    other_w = (1 - d) * 32
 
     loads = [
         pltpu.make_async_copy(tok_hbm, tok, lsem.at[0]),
@@ -132,17 +141,11 @@
     for p in partners:
         pl.semaphore_signal(barrier, inc=1, device_id=p, device_id_type=MESH)
 
-    loads[0].wait()
-
     def square(i, a):
         for u in range(4):
             v = tok[:, lanes(i * 4 + u)].astype(F32)
             a = a + v * v
         return a
-
-    total = lax.fori_loop(0, RT // 4, square, jnp.zeros((32, 128), F32))
-    inv_rms = lax.rsqrt(jnp.sum(total, axis=1, keepdims=True) * (1.0 / 4096.0) + 1e-05)
-    inv[...] = jnp.broadcast_to(inv_rms, (32, 128))
 
     def norm(i, _):
         for u in range(4):
@@ -152,7 +155,10 @@
             x_all[t, rt] = (v * gain[pl.ds(rt, 1), :]).astype(BF16)
         return 0
 
-    lax.fori_loop(0, RT // 4, norm, 0)
+    loads[0].wait()
+    total = lax.fori_loop(0, RT // 4, square, jnp.zeros((32, 128), F32))
+    inv_rms = lax.rsqrt(jnp.sum(total, axis=1, keepdims=True) * (1.0 / 4096.0) + 1e-05)
+    inv[...] = jnp.broadcast_to(inv_rms, (32, 128))
     loads[1].wait()
     loads[2].wait()
     pl.semaphore_wait(barrier, len(partners))
@@ -168,49 +174,56 @@
     def x_chunk(c, q):
         return x_all.at[c, pl.ds(q * 8, 8)]
 
+    xz, xfwd = [], []
+
+    def x_over(q):
+        xz.append(net.send(x_chunk(t, q), x_chunk(t, q), other_half))
+
+    def forward(q):
+        net.recv(xz[q], x_chunk(oc, q))
+        xfwd.append([net.send(x_chunk(oc, q), x_chunk(oc, q), x_peer(k)) for k in (1, 2, 3)])
+
     wz = [net.send(w_at(own_w, 0, 1), w_at(own_w, 1, 1), z4)]
     wy = [w_to_y(0, 1)]
-    xz = [net.send(x_chunk(t, 0), x_chunk(t, 0), other_half)]
+    lax.fori_loop(0, RT // 4, norm, 0)
+    if X_OVER[0] == 0:
+        x_over(0)
     xown = [net.send(x_all.at[t], x_all.at[t], x_peer(k)) for k in (1, 2, 3)]
-    xz.append(net.send(x_chunk(t, 1), x_chunk(t, 1), other_half))
-
+
+    net.recv(wz[0], w_at(own_w, 1, 1))
+    wz.append(net.send(w_at(own_w, 0, 2), w_at(own_w, 2, 2), z2))
+    wy.append(w_to_y(1, 1))
+    for q in range(4):
+        if X_OVER[q] == 1:
+            x_over(q)
     slot_tables(rows[...], cols[...], counts[...], zl, table)
     to_smem = pltpu.make_async_copy(table, sm, lsem.at[4])
     to_smem.start()
 
-    net.recv(wz[0], w_at(own_w, 1, 1))
-    wz.append(net.send(w_at(own_w, 0, 2), w_at(own_w, 2, 2), z2))
-    wy.append(w_to_y(1, 1))
-
+    net.recv(wz[1], w_at(own_w, 2, 2))
+    wz.append(net.send(w_at(own_w, 0, 4), w_at(own_w, 4, 4), z1))
+    wy.append(w_to_y(2, 2))
+    for q in range(4):
+        if X_OVER[q] == 2:
+            x_over(q)
     loads[3].wait()
     for c in range(CT):
         v = go[:, c * 128 : (c + 1) * 128]
         gs[c] = v
         gt[c] = v.T
 
-    net.recv(wz[1], w_at(own_w, 2, 2))
-    wz.append(net.send(w_at(own_w, 0, 4), w_at(own_w, 4, 4), z1))
-    wy.append(w_to_y(2, 2))
-    xz.append(net.send(x_chunk(t, 2), x_chunk(t, 2), other_half))
-    xz.append(net.send(x_chunk(t, 3), x_chunk(t, 3), other_half))
-
-    xfwd = []
-
-    def forward(q):
-        net.recv(xz[q], x_chunk(oc, q))
-        xfwd.append([net.send(x_chunk(oc, q), x_chunk(oc, q), x_peer(k)) for k in (1, 2, 3)])
-
     net.recv(wz[2], w_at(own_w, 4, 4))
     wy.append(w_to_y(4, 4))
     wc = [net.send(w_at(own_w, 1, 7), w_at(own_w, 1, 7), core)]
+    for q in range(4):
+        if X_OVER[q] == 3:
+            x_over(q)
     forward(0)
     for k in (1, 2, 3):
         base = d * 32 + lax.rem(y + 4 - k, 4) * 8
         for ids, (lo, n) in zip(wy, ((0, 1), (1, 1), (2, 2), (4, 4))):
             net.recv(ids[k - 1], w_at(base, lo, n))
         wc.append(net.send(w_at(base, 0, 8), w_at(base, 0, 8), core))
-    forward(1)
-    other_w = (1 - d) * 32
     net.recv(wc[0], w_at(other_w + y * 8, 1, 7))
     for k in (1, 2, 3):
         net.recv(wc[k], w_at(other_w + lax.rem(y + 4 - k, 4) * 8, 0, 8))
@@ -245,10 +258,6 @@
     for q in range(4):
         assemble(q)
         rs_other.append(scatter(1 - h, 0, q))
-    forward(2)
-    for q in range(4):
-        rs_own.append(scatter(h, 1, q))
-    forward(3)
 
     zids = []
 
@@ -266,51 +275,54 @@
         part = pl.ds(q * 8, 8)
         zids.append(net.send(zs.at[part], zr.at[part], other_half))
 
+    forward(1)
+    forward(2)
+    reduce_other(0)
+    forward(3)
+    reduce_other(1)
+    reduce_other(2)
+    reduce_other(3)
+    for q in range(4):
+        rs_own.append(scatter(h, 1, q))
     for k in (1, 2, 3):
         net.recv(xown[k - 1], x_all.at[h * 4 + lax.rem(x + 4 - k, 4)])
-    reduce_other(0)
-    reduce_other(1)
-    for k in (1, 2, 3):
         for q in range(4):
             net.recv(xfwd[q][k - 1], x_chunk((1 - h) * 4 + lax.rem(x + 4 - k, 4), q))
 
-    def tile_grad(j, yy, out, cast):
+    def tile_grad(first, out, at, cast):
         def one(q, _):
-            p = j * 32 + yy * 8 + q
+            p = first + q
             xs = x_all[:, sm[10, p]].reshape(256, 128)
-            out[yy * 8 + q] = jnp.dot(gt[sm[11, p]], xs, preferred_element_type=F32).astype(cast)
+            out[at + q] = jnp.dot(gt[sm[11, p]], xs, preferred_element_type=F32).astype(cast)
             return 0
 
-        lax.fori_loop(0, 8, one, 0, unroll=True)
-
-    def tiles8(ref, yy):
-        return ref.at[pl.ds(yy * 8, 8)]
-
-    dc = {}
-    for k in (1, 2, 3, 0):
-        yy = lax.rem(y + k, 4)
-        tile_grad(1 - d, yy, dt, BF16)
-        dc[k] = net.send(tiles8(dt, yy), tiles8(dr, yy), core)
-    reduce_other(2)
-    reduce_other(3)
-    ty = {}
-    for k in (1, 2, 3, 0):
-        yy = lax.rem(y + k, 4)
-        tile_grad(d, yy, e, F32)
-        net.recv(dc[k], tiles8(dr, yy))
+        lax.fori_loop(0, 4, one, 0, unroll=True)
+
+    def tiles4(ref, at):
+        return ref.at[pl.ds(at, 4)]
+
+    order = [(lo, k) for lo in (4, 0) for k in (1, 2, 3, 0)]
+    dc, ty = {}, {}
+    for lo, k in order:
+        at = lax.rem(y + k, 4) * 8 + lo
+        tile_grad(other_w + at, dt, at, BF16)
+        dc[lo, k] = net.send(tiles4(dt, at), tiles4(dr, at), core)
+    for lo, k in order:
+        at = lax.rem(y + k, 4) * 8 + lo
+        tile_grad(d * 32 + at, e, at, F32)
+        net.recv(dc[lo, k], tiles4(dr, at))
 
         def join(q, _):
-            i = yy * 8 + q
-            v = e[i] + dr[i].astype(F32)
+            v = e[at + q] + dr[at + q].astype(F32)
             if k:
-                es[i] = v.astype(BF16)
+                es[at + q] = v.astype(BF16)
             else:
-                e[i] = v
+                e[at + q] = v
             return 0
 
-        lax.fori_loop(0, 8, join, 0)
+        lax.fori_loop(0, 4, join, 0)
         if k:
-            ty[k] = net.send(tiles8(es, yy), yr.at[k - 1], y_peer(k))
+            ty[lo, k] = net.send(tiles4(es, at), yr.at[k - 1, pl.ds(lo, 4)], y_peer(k))
 
     def gain_part(rt, _):
         v = s[:, rt].astype(F32) * x_all[:, rt].astype(F32)
@@ -318,7 +330,11 @@
         return 0
 
     lax.fori_loop(0, RT, gain_part, 0)
-    gid = net.send(gp.at[pl.ds((1 - d) * 16, 16)], gc, core)
+
+    def piece(dd, k):
+        return lax.rem(d + dd, 2) * 16 + lax.rem(x + k, 4) * 4
+
+    gids = [net.send(gp.at[pl.ds(piece(dd, k), 4)], gc.at[i], x_peer(k, dd)) for i, (dd, k) in enumerate(plane)]
 
     def ahead(b, acc):
         for u in range(4):
@@ -329,53 +345,43 @@
             pf[i] = acc.astype(BF16)
         return acc
 
-    lax.fori_loop(0, SLOTS // 4, ahead, jnp.zeros((256, 128), F32))
+    acc = lax.fori_loop(0, SLOTS // 8, ahead, jnp.zeros((256, 128), F32))
+    mine = d * 16 + x * 4
+    for i in range(7):
+        net.recv(gids[i], gc.at[i])
+    for i in range(4):
+        v = gp[mine + i]
+        for k in range(7):
+            v = v + gc[k, i]
+        gy[y, i] = v
+    gids = [net.send(gy.at[y], gy.at[y], y_peer(k)) for k in (1, 2, 3)]
+
+    lax.fori_loop(SLOTS // 8, SLOTS // 4, ahead, acc)
     for c in range(CT):
         v = pf[sm[8, c]].astype(F32) * sm[9, c].astype(F32)
         mx[:, c * 128 : (c + 1) * 128] = v.astype(BF16)
     mixed_out = pltpu.make_async_copy(mx, mixed_hbm, lsem.at[5])
     mixed_out.start()
 
-    net.recv(gid, gc)
-    for i in range(16):
-        g1[i] = gp[d * 16 + i] + gc[i]
-    gids = [net.send(g1.at[pl.ds(lax.rem(x + k, 4) * 4, 4)], gx4.at[k - 1], x_peer(k)) for k in (1, 2, 3)]
-
-    for k in (1, 2, 3):
-        for q in range(4):
-            net.recv(rs_own[q][k - 1], r.at[1, k - 1, pl.ds(q * 8, 8)])
-
-    def own(rt, _):
-        v = s[t, rt].astype(F32) + r[1, 0, rt].astype(F32)
-        ig[rt] = v + r[1, 1, rt].astype(F32) + r[1, 2, rt].astype(F32)
-        return 0
-
-    lax.fori_loop(0, RT, own, 0)
-
-    for k in (1, 2, 3):
-        net.recv(gids[k - 1], gx4.at[k - 1])
+    for k in (1, 2, 3):
+        net.recv(gids[k - 1], gy.at[lax.rem(y + 4 - k, 4)])
     for i in range(4):
-        gy[y, i] = g1[x * 4 + i] + gx4[0, i] + gx4[1, i] + gx4[2, i]
-    gids = [net.send(gy.at[y], gy.at[y], y_peer(k)) for k in (1, 2, 3)]
-
-    for k in (1, 2, 3):
-        net.recv(ty[k], yr.at[k - 1])
+        gz[z, i] = gy[0, i] + gy[1, i] + gy[2, i] + gy[3, i]
+    gids = [net.send(gz.at[z], gz.at[z], z_peer(k)) for k in range(1, 16)]
 
     def sum_y(q):
         v = e[y * 8 + q] + yr[0, q].astype(F32)
         return v + yr[1, q].astype(F32) + yr[2, q].astype(F32)
 
+    for k in (1, 2, 3):
+        net.recv(ty[4, k], yr.at[k - 1, pl.ds(4, 4)])
     for q in range(4, 8):
         fs[q] = sum_y(q).astype(BF16)
     tz1 = net.send(fs.at[pl.ds(4, 4)], fr.at[pl.ds(4, 4)], z1)
+    for k in (1, 2, 3):
+        net.recv(ty[0, k], yr.at[k - 1, pl.ds(0, 4)])
     for q in range(4):
         fa[q] = sum_y(q)
-
-    for k in (1, 2, 3):
-        net.recv(gids[k - 1], gy.at[lax.rem(y + 4 - k, 4)])
-    for i in range(4):
-        gh[0, i] = gy[0, i] + gy[1, i] + gy[2, i] + gy[3, i]
-    gid = net.send(gh.at[0], gh.at[1], other_half)
 
     net.recv(tz1, fr.at[pl.ds(4, 4)])
     for q in (2, 3):
@@ -384,20 +390,30 @@
     for q in (0, 1):
         fa[q] = fa[q] + fr[q + 4].astype(F32)
 
-    net.recv(gid, gh.at[1])
-    for i in range(4):
-        gz[0, i] = gh[0, i] + gh[1, i]
-    gid = net.send(gz.at[0], gz.at[1], z4)
+    for k in (1, 2, 3):
+        for q in range(4):
+            net.recv(rs_own[q][k - 1], r.at[1, k - 1, pl.ds(q * 8, 8)])
+
+    def own(rt, _):
+        v = s[t, rt].astype(F32) + r[1, 0, rt].astype(F32)
+        ig[rt] = v + r[1, 1, rt].astype(F32) + r[1, 2, rt].astype(F32)
+        return 0
+
+    lax.fori_loop(0, RT, own, 0)
 
     net.recv(tz2, fr.at[pl.ds(2, 2)])
     fs[1] = (fa[1] + fr[3].astype(F32)).astype(BF16)
     tz3 = net.send(fs.at[pl.ds(1, 1)], fr.at[pl.ds(1, 1)], z4)
     fa[0] = fa[0] + fr[2].astype(F32)
 
-    net.recv(gid, gz.at[1])
+    for k in range(1, 16):
+        net.recv(gids[k - 1], gz.at[lax.rem(z + 16 - k, 16)])
     for i in range(4):
-        gz[2, i] = gz[0, i] + gz[1, i]
-    gid = net.send(gz.at[2], gz.at[3], z2)
+        v = gz[0, i]
+        for k in range(1, 16):
+            v = v + gz[k, i]
+        ga[mine + i] = v / gain[pl.ds(mine + i, 1), :]
+    gids = [net.send(ga.at[pl.ds(mine, 4)], ga.at[pl.ds(mine, 4)], x_peer(k, dd)) for dd, k in plane]
 
     def hidden(rt, a):
         v = (ig[rt] + zr[rt].astype(F32)) * gain[pl.ds(rt, 1), :]
@@ -405,30 +421,9 @@
         return a + v * scaled[rt]
 
     acc = jnp.zeros((32, 128), F32)
-    for q in range(2):
+    for q in range(4):
         net.recv(zids[q], zr.at[pl.ds(q * 8, 8)])
         acc = lax.fori_loop(q * 8, q * 8 + 8, hidden, acc)
-
-    net.recv(gid, gz.at[3])
-    for i in range(4):
-        gz[4, i] = gz[2, i] + gz[3, i]
-    gid = net.send(gz.at[4], gz.at[5], z1)
-
-    net.recv(tz3, fr.at[pl.ds(1, 1)])
-    keep = jnp.where(counts_s[0, f] > d, 1.0, 0.0)
-    tiles[d] = (fa[0] + fr[1].astype(F32)).T * keep
-    tc = net.send(tiles.at[d], tiles.at[d], core)
-
-    for q in range(2, 4):
-        net.recv(zids[q], zr.at[pl.ds(q * 8, 8)])
-        acc = lax.fori_loop(q * 8, q * 8 + 8, hidden, acc)
-
-    net.recv(gid, gz.at[5])
-    mine = d * 16 + x * 4
-    for i in range(4):
-        ga[mine + i] = (gz[4, i] + gz[5, i]) / gain[pl.ds(mine + i, 1), :]
-    gids = [net.send(ga.at[pl.ds(mine, 4)], ga.at[pl.ds(mine, 4)], x_peer(k)) for k in (1, 2, 3)]
-
     mean = jnp.sum(acc, axis=1, keepdims=True) * (1.0 / 4096.0)
 
     def finish(i, _):
@@ -442,15 +437,18 @@
     gx_out = pltpu.make_async_copy(ox, gx_hbm, lsem.at[6])
     gx_out.start()
 
-    for k in (1, 2, 3):
-        net.recv(gids[k - 1], ga.at[pl.ds(d * 16 + lax.rem(x + 4 - k, 4) * 4, 4)])
-    gid = net.send(ga.at[pl.ds(d * 16, 16)], ga.at[pl.ds(d * 16, 16)], core)
+    net.recv(tz3, fr.at[pl.ds(1, 1)])
+    keep = jnp.where(counts_s[0, f] > d, 1.0, 0.0)
+    tiles[d] = (fa[0] + fr[1].astype(F32)).T * keep
+    tc = net.send(tiles.at[d], tiles.at[d], core)
+
+    for i, (dd, k) in enumerate(plane):
+        net.recv(gids[i], ga.at[pl.ds(piece(dd, 4 - k), 4)])
+    gg_out = pltpu.make_async_copy(ga, gg_hbm, lsem.at[8])
+    gg_out.start()
     net.recv(tc, tiles.at[1 - d])
     gt_out = pltpu.make_async_copy(tiles, gt_hbm, lsem.at[7])
     gt_out.start()
-    net.recv(gid, ga.at[pl.ds((1 - d) * 16, 16)])
-    gg_out = pltpu.make_async_copy(ga, gg_hbm, lsem.at[8])
-    gg_out.start()
     for copy in net.sent:
         copy.wait_send()
     for copy in (mixed_out, gx_out, gt_out, gg_out):
@@ -504,19 +502,16 @@
             pltpu.VMEM((16, 128), jnp.int32),
             pltpu.SMEM((16, 128), jnp.int32),
             pltpu.VMEM((RT, 1, 128), F32),
-            pltpu.VMEM((16, 1, 128), F32),
-            pltpu.VMEM((16, 1, 128), F32),
-            pltpu.VMEM((3, 4, 1, 128), F32),
+            pltpu.VMEM((7, 4, 1, 128), F32),
             pltpu.VMEM((4, 4, 1, 128), F32),
-            pltpu.VMEM((2, 4, 1, 128), F32),
-            pltpu.VMEM((6, 4, 1, 128), F32),
+            pltpu.VMEM((16, 4, 1, 128), F32),
             pltpu.VMEM((RT, 1, 128), F32),
             pltpu.SemaphoreType.DMA((NSEM,)),
             pltpu.SemaphoreType.DMA((NSEM,)),
             pltpu.SemaphoreType.DMA((9,)),
         ],
         compiler_params=pltpu.CompilerParams(
-            collective_id=0, has_side_effects=True, vmem_limit_bytes=52 * 1024 * 1024
+            collective_id=0, has_side_effects=True, vmem_limit_bytes=62 * 1024 * 1024
         ),
         name="sparse_mlp",
     )(

time: 138 us -> 120 us (0.87)
  the two profiles are of different devices: /device:TPU:1 before, /device:TPU:41 now
where the time goes in v2:
time: 120 us
  Pallas kernels  115 us (96%)
  local copies, waits for them, and re-layouts  4.19 us (3%)
    pallas_call x1, Pallas kernels, per_device(): pl.pallas_call(kernel, out_shape=(jax.ShapeDtypeStruct((256, 1792), BF16)...  115 us
    unnamed x10, local copies, waits for them, and re-layouts  4.19 us

profile of v2, /device:TPU:41, one launch (start us, length us, event | category | flops | bytes accessed | tf_op | source)
XLA Modules:
  0.0 120.0 jit_solution(13981242878503565023)
XLA Ops:
  0.6 115.1 %sparse_mlp.1 = (bf16[256,1792]{1,0:T(8,128)(2,1)}, bf16[32,4096]{1,0:T(8,128)(2,1)}, f32[32,1,128]{2,1,0:T(1,128)}, f32[2,128,128]{2,1,0:T(8,128)}) custom-call(bf16[32,4096]{1,0:T(8,128)(2,1)} %tok_hbm.1, f32[32,128]{1,0:T(8,128)} %bitcast.2, bf16[2,128,128]{2,1,0:T(8,128)(2,1)} %tv_hbm.1, s32[1,64]{1,0:T(1,128)} %rows.1, s32[1,64]{1,0:T(1,128)} %cols.1, ...), custom_call_target="tpu_custom_call" | custom-call | tf_op jit(solution)/shard_map/sparse_mlp/pallas_call | solution.py:465
  115.8 0.0 copy-start
  115.8 2.2 %copy.15 = bf16[256,1792]{1,0:T(8,128)(2,1)} copy(bf16[256,1792]{1,0:T(8,128)(2,1)} %get-tuple-element.16) | data formatting | bytes 1835008
  118.0 0.0 copy-done
  118.0 0.0 copy-start.2
  118.0 0.0 copy-start.1
  118.0 0.7 copy.16
  118.7 0.0 copy-done.2
  118.7 0.6 copy.17
  119.3 0.0 copy-done.1
  119.3 0.7 copy.18
Async XLA Ops:
  115.8 2.2 %copy-start = (bf16[32,4096]{1,0:T(8,128)(2,1)S(1)}, bf16[32,4096]{1,0:T(8,128)(2,1)}, u32[]{:S(2)}) copy-start(bf16[32,4096]{1,0:T(8,128)(2,1)} %get-tuple-element.17) | copy-start | bytes 786436
  118.0 0.7 copy-start.2
  118.0 1.3 %copy-start.1 = (f32[2,128,128]{2,1,0:T(8,128)S(1)}, f32[2,128,128]{2,1,0:T(8,128)}, u32[]{:S(2)}) copy-start(f32[2,128,128]{2,1,0:T(8,128)} %get-tuple-element.19) | copy-start | bytes 393220

commit v3 on v2

--- a/solution.py
+++ b/solution.py
@@ -14,7 +14,9 @@
 CT = 14
 SLOTS = 64
 NSEM = 160
-X_OVER = (0, 2, 3, 3)
+X_OVER = (1, 2, 3, 3)
+FORWARD = (0, 1, 2, 3)
+TILES_AT = 2
 
 
 class Net:
@@ -183,11 +185,17 @@
         net.recv(xz[q], x_chunk(oc, q))
         xfwd.append([net.send(x_chunk(oc, q), x_chunk(oc, q), x_peer(k)) for k in (1, 2, 3)])
 
+    def forwards(at):
+        for q in range(4):
+            if FORWARD[q] == at:
+                forward(q)
+
     wz = [net.send(w_at(own_w, 0, 1), w_at(own_w, 1, 1), z4)]
     wy = [w_to_y(0, 1)]
     lax.fori_loop(0, RT // 4, norm, 0)
-    if X_OVER[0] == 0:
-        x_over(0)
+    for q in range(4):
+        if X_OVER[q] == 0:
+            x_over(q)
     xown = [net.send(x_all.at[t], x_all.at[t], x_peer(k)) for k in (1, 2, 3)]
 
     net.recv(wz[0], w_at(own_w, 1, 1))
@@ -195,39 +203,41 @@
     wy.append(w_to_y(1, 1))
     for q in range(4):
         if X_OVER[q] == 1:
+            x_over(q)
+
+    net.recv(wz[1], w_at(own_w, 2, 2))
+    wz.append(net.send(w_at(own_w, 0, 4), w_at(own_w, 4, 4), z1))
+    wy.append(w_to_y(2, 2))
+    for q in range(4):
+        if X_OVER[q] == 2:
+            x_over(q)
+
+    net.recv(wz[2], w_at(own_w, 4, 4))
+    wy.append(w_to_y(4, 4))
+    wc = [net.send(w_at(own_w, 1, 7), w_at(own_w, 1, 7), core)]
+    for q in range(4):
+        if X_OVER[q] == 3:
             x_over(q)
     slot_tables(rows[...], cols[...], counts[...], zl, table)
     to_smem = pltpu.make_async_copy(table, sm, lsem.at[4])
     to_smem.start()
-
-    net.recv(wz[1], w_at(own_w, 2, 2))
-    wz.append(net.send(w_at(own_w, 0, 4), w_at(own_w, 4, 4), z1))
-    wy.append(w_to_y(2, 2))
-    for q in range(4):
-        if X_OVER[q] == 2:
-            x_over(q)
     loads[3].wait()
     for c in range(CT):
         v = go[:, c * 128 : (c + 1) * 128]
         gs[c] = v
         gt[c] = v.T
-
-    net.recv(wz[2], w_at(own_w, 4, 4))
-    wy.append(w_to_y(4, 4))
-    wc = [net.send(w_at(own_w, 1, 7), w_at(own_w, 1, 7), core)]
-    for q in range(4):
-        if X_OVER[q] == 3:
-            x_over(q)
-    forward(0)
+    forwards(0)
     for k in (1, 2, 3):
         base = d * 32 + lax.rem(y + 4 - k, 4) * 8
         for ids, (lo, n) in zip(wy, ((0, 1), (1, 1), (2, 2), (4, 4))):
             net.recv(ids[k - 1], w_at(base, lo, n))
         wc.append(net.send(w_at(base, 0, 8), w_at(base, 0, 8), core))
+    forwards(1)
     net.recv(wc[0], w_at(other_w + y * 8, 1, 7))
     for k in (1, 2, 3):
         net.recv(wc[k], w_at(other_w + lax.rem(y + 4 - k, 4) * 8, 0, 8))
     to_smem.wait()
+    forwards(2)
 
     def back(b, acc):
         for u in range(4):
@@ -275,20 +285,6 @@
         part = pl.ds(q * 8, 8)
         zids.append(net.send(zs.at[part], zr.at[part], other_half))
 
-    forward(1)
-    forward(2)
-    reduce_other(0)
-    forward(3)
-    reduce_other(1)
-    reduce_other(2)
-    reduce_other(3)
-    for q in range(4):
-        rs_own.append(scatter(h, 1, q))
-    for k in (1, 2, 3):
-        net.recv(xown[k - 1], x_all.at[h * 4 + lax.rem(x + 4 - k, 4)])
-        for q in range(4):
-            net.recv(xfwd[q][k - 1], x_chunk((1 - h) * 4 + lax.rem(x + 4 - k, 4), q))
-
     def tile_grad(first, out, at, cast):
         def one(q, _):
             p = first + q
@@ -303,49 +299,42 @@
 
     order = [(lo, k) for lo in (4, 0) for k in (1, 2, 3, 0)]
     dc, ty = {}, {}
-    for lo, k in order:
-        at = lax.rem(y + k, 4) * 8 + lo
-        tile_grad(other_w + at, dt, at, BF16)
-        dc[lo, k] = net.send(tiles4(dt, at), tiles4(dr, at), core)
-    for lo, k in order:
-        at = lax.rem(y + k, 4) * 8 + lo
-        tile_grad(d * 32 + at, e, at, F32)
-        net.recv(dc[lo, k], tiles4(dr, at))
-
-        def join(q, _):
-            v = e[at + q] + dr[at + q].astype(F32)
-            if k:
-                es[at + q] = v.astype(BF16)
-            else:
-                e[at + q] = v
-            return 0
-
-        lax.fori_loop(0, 4, join, 0)
-        if k:
-            ty[lo, k] = net.send(tiles4(es, at), yr.at[k - 1, pl.ds(lo, 4)], y_peer(k))
+
+    def tiles_to_core():
+        for k in (1, 2, 3):
+            net.recv(xown[k - 1], x_all.at[h * 4 + lax.rem(x + 4 - k, 4)])
+            for q in range(4):
+                net.recv(xfwd[q][k - 1], x_chunk((1 - h) * 4 + lax.rem(x + 4 - k, 4), q))
+        for lo, k in order:
+            at = lax.rem(y + k, 4) * 8 + lo
+            tile_grad(other_w + at, dt, at, BF16)
+            dc[lo, k] = net.send(tiles4(dt, at), tiles4(dr, at), core)
 
     def gain_part(rt, _):
         v = s[:, rt].astype(F32) * x_all[:, rt].astype(F32)
         gp[rt] = jnp.sum(v.reshape(256, 128), axis=0, keepdims=True)
         return 0
 
-    lax.fori_loop(0, RT, gain_part, 0)
-
     def piece(dd, k):
         return lax.rem(d + dd, 2) * 16 + lax.rem(x + k, 4) * 4
 
-    gids = [net.send(gp.at[pl.ds(piece(dd, k), 4)], gc.at[i], x_peer(k, dd)) for i, (dd, k) in enumerate(plane)]
-
-    def ahead(b, acc):
-        for u in range(4):
-            i = b * 4 + u
-            xs = x_all[:, sm[6, i]].reshape(256, 128)
-            prod = jnp.dot(xs, w[sm[5, i]], preferred_element_type=F32)
-            acc = acc * sm[7, i].astype(F32) + prod
-            pf[i] = acc.astype(BF16)
-        return acc
-
-    acc = lax.fori_loop(0, SLOTS // 8, ahead, jnp.zeros((256, 128), F32))
+    gids = []
+
+    def gain_to_plane():
+        lax.fori_loop(0, RT, gain_part, 0)
+        for i, (dd, k) in enumerate(plane):
+            gids.append(net.send(gp.at[pl.ds(piece(dd, k), 4)], gc.at[i], x_peer(k, dd)))
+
+    forwards(3)
+    for q in range(4):
+        if TILES_AT == q:
+            tiles_to_core()
+            gain_to_plane()
+        reduce_other(q)
+        forwards(4 + q)
+    if TILES_AT == 4:
+        tiles_to_core()
+        gain_to_plane()
     mine = d * 16 + x * 4
     for i in range(7):
         net.recv(gids[i], gc.at[i])
@@ -356,7 +345,36 @@
         gy[y, i] = v
     gids = [net.send(gy.at[y], gy.at[y], y_peer(k)) for k in (1, 2, 3)]
 
-    lax.fori_loop(SLOTS // 8, SLOTS // 4, ahead, acc)
+    for lo, k in order:
+        at = lax.rem(y + k, 4) * 8 + lo
+        tile_grad(d * 32 + at, e, at, F32)
+        net.recv(dc[lo, k], tiles4(dr, at))
+
+        def join(q, _):
+            v = e[at + q] + dr[at + q].astype(F32)
+            if k:
+                es[at + q] = v.astype(BF16)
+            else:
+                e[at + q] = v
+            return 0
+
+        lax.fori_loop(0, 4, join, 0)
+        if k:
+            ty[lo, k] = net.send(tiles4(es, at), yr.at[k - 1, pl.ds(lo, 4)], y_peer(k))
+
+    for q in range(4):
+        rs_own.append(scatter(h, 1, q))
+
+    def ahead(b, acc):
+        for u in range(4):
+            i = b * 4 + u
+            xs = x_all[:, sm[6, i]].reshape(256, 128)
+            prod = jnp.dot(xs, w[sm[5, i]], preferred_element_type=F32)
+            acc = acc * sm[7, i].astype(F32) + prod
+            pf[i] = acc.astype(BF16)
+        return acc
+
+    lax.fori_loop(0, SLOTS // 4, ahead, jnp.zeros((256, 128), F32))
     for c in range(CT):
         v = pf[sm[8, c]].astype(F32) * sm[9, c].astype(F32)
         mx[:, c * 128 : (c + 1) * 128] = v.astype(BF16)
@@ -455,6 +473,19 @@
         copy.wait()
 
 
+def outward(*refs):
+    made, outs, held, (sem_in, sem_out) = refs[:4], refs[4:8], refs[8:12], refs[12:]
+    into = [pltpu.make_async_copy(a, v, sem_in.at[i]) for i, (a, v) in enumerate(zip(made, held))]
+    out = [pltpu.make_async_copy(v, o, sem_out.at[i]) for i, (v, o) in enumerate(zip(held, outs))]
+    for c in into:
+        c.start()
+    for c, o in zip(into, out):
+        c.wait()
+        o.start()
+    for o in out:
+        o.wait()
+
+
 def per_device(tokens, norm_gain, tile_values, tile_rows, tile_cols, tile_counts, grad_out):
     hbm = pl.BlockSpec(memory_space=pl.ANY)
     vmem = pl.BlockSpec(memory_space=pltpu.VMEM)
@@ -462,14 +493,15 @@
     rows8 = (8, RT, 32, 128)
     local = (RT, 32, 128)
     tiles32 = (32, 128, 128)
-    mixed, grad_x, grad_gain, grad_tiles = pl.pallas_call(
+    shapes = (
+        jax.ShapeDtypeStruct((256, 1792), BF16),
+        jax.ShapeDtypeStruct((32, 4096), BF16),
+        jax.ShapeDtypeStruct((RT, 1, 128), F32),
+        jax.ShapeDtypeStruct((2, 128, 128), F32),
+    )
+    made = pl.pallas_call(
         kernel,
-        out_shape=(
-            jax.ShapeDtypeStruct((256, 1792), BF16),
-            jax.ShapeDtypeStruct((32, 4096), BF16),
-            jax.ShapeDtypeStruct((RT, 1, 128), F32),
-            jax.ShapeDtypeStruct((2, 128, 128), F32),
-        ),
+        out_shape=shapes,
         in_specs=[hbm, vmem, hbm, vmem, vmem, vmem, smem, hbm],
         out_specs=(hbm, hbm, hbm, hbm),
         scratch_shapes=[
@@ -518,6 +550,14 @@
         tokens, norm_gain.reshape(RT, 128), tile_values, tile_rows, tile_cols, tile_counts,
         tile_counts, grad_out,
     )
+    mixed, grad_x, grad_gain, grad_tiles = pl.pallas_call(
+        outward,
+        out_shape=shapes,
+        in_specs=[hbm] * 4,
+        out_specs=(hbm,) * 4,
+        scratch_shapes=[pltpu.VMEM(a.shape, a.dtype) for a in shapes] + [pltpu.SemaphoreType.DMA((4,))] * 2,
+        name="outward",
+    )(*made)
     return mixed, grad_x, grad_gain.reshape(4096), grad_tiles
 
 

time: 120 us -> 110 us (0.917)
  the two profiles are of different devices: /device:TPU:41 before, /device:TPU:1 now
where the time goes in v3:
time: 110 us
  Pallas kernels  109 us (99%)
    pallas_call x1, Pallas kernels, per_device(): pl.pallas_call(kernel, out_shape=shapes, in_specs=[hbm, vmem, hbm, vmem,...  107 us
    pallas_call x1, Pallas kernels, per_device(): pl.pallas_call(outward, out_shape=shapes, in_specs=[hbm] * 4, out_specs=(...  2.3 us

profile of v3, /device:TPU:1, one launch (start us, length us, event | category | flops | bytes accessed | tf_op | source)
XLA Modules:
  0.0 110.1 jit_solution(6178191440227257140)
XLA Ops:
  0.6 107.2 %sparse_mlp.1 = (bf16[256,1792]{1,0:T(8,128)(2,1)}, bf16[32,4096]{1,0:T(8,128)(2,1)}, f32[32,1,128]{2,1,0:T(1,128)}, f32[2,128,128]{2,1,0:T(8,128)}) custom-call(bf16[32,4096]{1,0:T(8,128)(2,1)} %tok_hbm.1, f32[32,128]{1,0:T(8,128)} %bitcast.2, bf16[2,128,128]{2,1,0:T(8,128)(2,1)} %tv_hbm.1, s32[1,64]{1,0:T(1,128)} %rows.1, s32[1,64]{1,0:T(1,128)} %cols.1, ...), custom_call_target="tpu_custom_call" | custom-call | tf_op jit(solution)/shard_map/sparse_mlp/pallas_call | solution.py:502
  107.8 2.3 %outward.1 = (bf16[256,1792]{1,0:T(8,128)(2,1)}, bf16[32,4096]{1,0:T(8,128)(2,1)}, f32[32,1,128]{2,1,0:T(1,128)}, f32[2,128,128]{2,1,0:T(8,128)}) custom-call(bf16[256,1792]{1,0:T(8,128)(2,1)} %get-tuple-element.12.refs_0_, bf16[32,4096]{1,0:T(8,128)(2,1)} %get-tuple-element.13.refs_1_, f32[32,1,128]{2,1,0:T(1,128)} %get-tuple-element.14.refs_2_, ...), custom_call_target="tpu_custom_call" | custom-call | tf_op jit(solution)/shard_map/outward/pallas_call | solution.py:553

commit v4 on v3

--- a/solution.py
+++ b/solution.py
@@ -16,6 +16,8 @@
 NSEM = 160
 X_OVER = (1, 2, 3, 3)
 FORWARD = (0, 1, 2, 3)
+NORM_FIRST = True
+OWN_AT = (4, 4, 4, 4)
 TILES_AT = 2
 
 
@@ -161,6 +163,8 @@
     total = lax.fori_loop(0, RT // 4, square, jnp.zeros((32, 128), F32))
     inv_rms = lax.rsqrt(jnp.sum(total, axis=1, keepdims=True) * (1.0 / 4096.0) + 1e-05)
     inv[...] = jnp.broadcast_to(inv_rms, (32, 128))
+    if NORM_FIRST:
+        lax.fori_loop(0, RT // 4, norm, 0)
     loads[1].wait()
     loads[2].wait()
     pl.semaphore_wait(barrier, len(partners))
@@ -192,7 +196,8 @@
 
     wz = [net.send(w_at(own_w, 0, 1), w_at(own_w, 1, 1), z4)]
     wy = [w_to_y(0, 1)]
-    lax.fori_loop(0, RT // 4, norm, 0)
+    if not NORM_FIRST:
+        lax.fori_loop(0, RT // 4, norm, 0)
     for q in range(4):
         if X_OVER[q] == 0:
             x_over(q)
@@ -325,17 +330,58 @@
         for i, (dd, k) in enumerate(plane):
             gids.append(net.send(gp.at[pl.ds(piece(dd, k), 4)], gc.at[i], x_peer(k, dd)))
 
+    def own_sends(at):
+        for q in range(4):
+            if OWN_AT[q] == at:
+                rs_own.append(scatter(h, 1, q))
+
     forwards(3)
     for q in range(4):
         if TILES_AT == q:
             tiles_to_core()
-            gain_to_plane()
         reduce_other(q)
         forwards(4 + q)
+        own_sends(q)
     if TILES_AT == 4:
         tiles_to_core()
-        gain_to_plane()
     mine = d * 16 + x * 4
+
+    for lo, k in order:
+        at = lax.rem(y + k, 4) * 8 + lo
+        tile_grad(d * 32 + at, e, at, F32)
+        net.recv(dc[lo, k], tiles4(dr, at))
+
+        def join(q, _):
+            v = e[at + q] + dr[at + q].astype(F32)
+            if k:
+                es[at + q] = v.astype(BF16)
+            else:
+                e[at + q] = v
+            return 0
+
+        lax.fori_loop(0, 4, join, 0)
+        if k:
+            ty[lo, k] = net.send(tiles4(es, at), yr.at[k - 1, pl.ds(lo, 4)], y_peer(k))
+
+    gain_to_plane()
+    own_sends(4)
+
+    def ahead(b, acc):
+        for u in range(4):
+            i = b * 4 + u
+            xs = x_all[:, sm[6, i]].reshape(256, 128)
+            prod = jnp.dot(xs, w[sm[5, i]], preferred_element_type=F32)
+            acc = acc * sm[7, i].astype(F32) + prod
+            pf[i] = acc.astype(BF16)
+        return acc
+
+    lax.fori_loop(0, SLOTS // 4, ahead, jnp.zeros((256, 128), F32))
+    for c in range(CT):
+        v = pf[sm[8, c]].astype(F32) * sm[9, c].astype(F32)
+        mx[:, c * 128 : (c + 1) * 128] = v.astype(BF16)
+    mixed_out = pltpu.make_async_copy(mx, mixed_hbm, lsem.at[5])
+    mixed_out.start()
+
     for i in range(7):
         net.recv(gids[i], gc.at[i])
     for i in range(4):
@@ -345,48 +391,6 @@
         gy[y, i] = v
     gids = [net.send(gy.at[y], gy.at[y], y_peer(k)) for k in (1, 2, 3)]
 
-    for lo, k in order:
-        at = lax.rem(y + k, 4) * 8 + lo
-        tile_grad(d * 32 + at, e, at, F32)
-        net.recv(dc[lo, k], tiles4(dr, at))
-
-        def join(q, _):
-            v = e[at + q] + dr[at + q].astype(F32)
-            if k:
-                es[at + q] = v.astype(BF16)
-            else:
-                e[at + q] = v
-            return 0
-
-        lax.fori_loop(0, 4, join, 0)
-        if k:
-            ty[lo, k] = net.send(tiles4(es, at), yr.at[k - 1, pl.ds(lo, 4)], y_peer(k))
-
-    for q in range(4):
-        rs_own.append(scatter(h, 1, q))
-
-    def ahead(b, acc):
-        for u in range(4):
-            i = b * 4 + u
-            xs = x_all[:, sm[6, i]].reshape(256, 128)
-            prod = jnp.dot(xs, w[sm[5, i]], preferred_element_type=F32)
-            acc = acc * sm[7, i].astype(F32) + prod
-            pf[i] = acc.astype(BF16)
-        return acc
-
-    lax.fori_loop(0, SLOTS // 4, ahead, jnp.zeros((256, 128), F32))
-    for c in range(CT):
-        v = pf[sm[8, c]].astype(F32) * sm[9, c].astype(F32)
-        mx[:, c * 128 : (c + 1) * 128] = v.astype(BF16)
-    mixed_out = pltpu.make_async_copy(mx, mixed_hbm, lsem.at[5])
-    mixed_out.start()
-
-    for k in (1, 2, 3):
-        net.recv(gids[k - 1], gy.at[lax.rem(y + 4 - k, 4)])
-    for i in range(4):
-        gz[z, i] = gy[0, i] + gy[1, i] + gy[2, i] + gy[3, i]
-    gids = [net.send(gz.at[z], gz.at[z], z_peer(k)) for k in range(1, 16)]
-
     def sum_y(q):
         v = e[y * 8 + q] + yr[0, q].astype(F32)
         return v + yr[1, q].astype(F32) + yr[2, q].astype(F32)
@@ -400,6 +404,12 @@
         net.recv(ty[0, k], yr.at[k - 1, pl.ds(0, 4)])
     for q in range(4):
         fa[q] = sum_y(q)
+
+    for k in (1, 2, 3):
+        net.recv(gids[k - 1], gy.at[lax.rem(y + 4 - k, 4)])
+    for i in range(4):
+        gz[z, i] = gy[0, i] + gy[1, i] + gy[2, i] + gy[3, i]
+    gids = [net.send(gz.at[z], gz.at[z], z_peer(k)) for k in range(1, 16)]
 
     net.recv(tz1, fr.at[pl.ds(4, 4)])
     for q in (2, 3):

time: 110 us -> 107 us (0.973)
  Pallas kernels: 109 us -> 106 us
    pallas_call x1, Pallas kernels: 107 us -> 104 us  [per_device(): pl.pallas_call(kernel, out_shape=shapes, in_specs=[hbm, vmem, hbm, vmem,...]
where the time goes in v4:
time: 107 us
  Pallas kernels  106 us (99%)
    pallas_call x1, Pallas kernels, per_device(): pl.pallas_call(kernel, out_shape=shapes, in_specs=[hbm, vmem, hbm, vmem,...  104 us
    pallas_call x1, Pallas kernels, per_device(): pl.pallas_call(outward, out_shape=shapes, in_specs=[hbm] * 4, out_specs=(...  2.3 us

profile of v4, /device:TPU:1, one launch (start us, length us, event | category | flops | bytes accessed | tf_op | source)
XLA Modules:
  0.0 106.5 jit_solution(1756792507095724199)
XLA Ops:
  0.6 103.6 %sparse_mlp.1 = (bf16[256,1792]{1,0:T(8,128)(2,1)}, bf16[32,4096]{1,0:T(8,128)(2,1)}, f32[32,1,128]{2,1,0:T(1,128)}, f32[2,128,128]{2,1,0:T(8,128)}) custom-call(bf16[32,4096]{1,0:T(8,128)(2,1)} %tok_hbm.1, f32[32,128]{1,0:T(8,128)} %bitcast.2, bf16[2,128,128]{2,1,0:T(8,128)(2,1)} %tv_hbm.1, s32[1,64]{1,0:T(1,128)} %rows.1, s32[1,64]{1,0:T(1,128)} %cols.1, ...), custom_call_target="tpu_custom_call" | custom-call | tf_op jit(solution)/shard_map/sparse_mlp/pallas_call | solution.py:512
  104.2 2.3 %outward.1 = (bf16[256,1792]{1,0:T(8,128)(2,1)}, bf16[32,4096]{1,0:T(8,128)(2,1)}, f32[32,1,128]{2,1,0:T(1,128)}, f32[2,128,128]{2,1,0:T(8,128)}) custom-call(bf16[256,1792]{1,0:T(8,128)(2,1)} %get-tuple-element.12.refs_0_, bf16[32,4096]{1,0:T(8,128)(2,1)} %get-tuple-element.13.refs_1_, f32[32,1,128]{2,1,0:T(1,128)} %get-tuple-element.14.refs_2_, ...), custom_call_target="tpu_custom_call" | custom-call | tf_op jit(solution)/shard_map/outward/pallas_call | solution.py:563

commit v5 on v4

--- a/solution.py
+++ b/solution.py
@@ -346,7 +346,17 @@
         tiles_to_core()
     mine = d * 16 + x * 4
 
+    gain_to_plane()
     for lo, k in order:
+        if (lo, k) == (0, 1):
+            for i in range(7):
+                net.recv(gids[i], gc.at[i])
+            for i in range(4):
+                v = gp[mine + i]
+                for n in range(7):
+                    v = v + gc[n, i]
+                gy[y, i] = v
+            gids = [net.send(gy.at[y], gy.at[y], y_peer(n)) for n in (1, 2, 3)]
         at = lax.rem(y + k, 4) * 8 + lo
         tile_grad(d * 32 + at, e, at, F32)
         net.recv(dc[lo, k], tiles4(dr, at))
@@ -363,7 +373,6 @@
         if k:
             ty[lo, k] = net.send(tiles4(es, at), yr.at[k - 1, pl.ds(lo, 4)], y_peer(k))
 
-    gain_to_plane()
     own_sends(4)
 
     def ahead(b, acc):
@@ -382,14 +391,12 @@
     mixed_out = pltpu.make_async_copy(mx, mixed_hbm, lsem.at[5])
     mixed_out.start()
 
-    for i in range(7):
-        net.recv(gids[i], gc.at[i])
+
+    for k in (1, 2, 3):
+        net.recv(gids[k - 1], gy.at[lax.rem(y + 4 - k, 4)])
     for i in range(4):
-        v = gp[mine + i]
-        for k in range(7):
-            v = v + gc[k, i]
-        gy[y, i] = v
-    gids = [net.send(gy.at[y], gy.at[y], y_peer(k)) for k in (1, 2, 3)]
+        gz[z, i] = gy[0, i] + gy[1, i] + gy[2, i] + gy[3, i]
+    gids = [net.send(gz.at[z], gz.at[z], z_peer(k)) for k in range(1, 16)]
 
     def sum_y(q):
         v = e[y * 8 + q] + yr[0, q].astype(F32)
@@ -404,12 +411,6 @@
         net.recv(ty[0, k], yr.at[k - 1, pl.ds(0, 4)])
     for q in range(4):
         fa[q] = sum_y(q)
-
-    for k in (1, 2, 3):
-        net.recv(gids[k - 1], gy.at[lax.rem(y + 4 - k, 4)])
-    for i in range(4):
-        gz[z, i] = gy[0, i] + gy[1, i] + gy[2, i] + gy[3, i]
-    gids = [net.send(gz.at[z], gz.at[z], z_peer(k)) for k in range(1, 16)]
 
     net.recv(tz1, fr.at[pl.ds(4, 4)])
     for q in (2, 3):

time: 107 us -> 106 us (level)
  Pallas kernels: 106 us -> 104 us
    pallas_call x1, Pallas kernels: 104 us -> 102 us  [per_device(): pl.pallas_call(kernel, out_shape=shapes, in_specs=[hbm, vmem, hbm, vmem,...]
where the time goes in v5:
time: 106 us; the launch traced here: 105 us
  Pallas kernels  104 us (98%)
    pallas_call x1, Pallas kernels, per_device(): pl.pallas_call(kernel, out_shape=shapes, in_specs=[hbm, vmem, hbm, vmem,...  102 us
    pallas_call x1, Pallas kernels, per_device(): pl.pallas_call(outward, out_shape=shapes, in_specs=[hbm] * 4, out_specs=(...  2.3 us

profile of v5, /device:TPU:1, one launch (start us, length us, event | category | flops | bytes accessed | tf_op | source)
XLA Modules:
  0.0 104.7 jit_solution(10682045998130808159)
XLA Ops:
  0.6 101.8 %sparse_mlp.1 = (bf16[256,1792]{1,0:T(8,128)(2,1)}, bf16[32,4096]{1,0:T(8,128)(2,1)}, f32[32,1,128]{2,1,0:T(1,128)}, f32[2,128,128]{2,1,0:T(8,128)}) custom-call(bf16[32,4096]{1,0:T(8,128)(2,1)} %tok_hbm.1, f32[32,128]{1,0:T(8,128)} %bitcast.2, bf16[2,128,128]{2,1,0:T(8,128)(2,1)} %tv_hbm.1, s32[1,64]{1,0:T(1,128)} %rows.1, s32[1,64]{1,0:T(1,128)} %cols.1, ...), custom_call_target="tpu_custom_call" | custom-call | tf_op jit(solution)/shard_map/sparse_mlp/pallas_call | solution.py:513
  102.4 2.3 %outward.1 = (bf16[256,1792]{1,0:T(8,128)(2,1)}, bf16[32,4096]{1,0:T(8,128)(2,1)}, f32[32,1,128]{2,1,0:T(1,128)}, f32[2,128,128]{2,1,0:T(8,128)}) custom-call(bf16[256,1792]{1,0:T(8,128)(2,1)} %get-tuple-element.12.refs_0_, bf16[32,4096]{1,0:T(8,128)(2,1)} %get-tuple-element.13.refs_1_, f32[32,1,128]{2,1,0:T(1,128)} %get-tuple-element.14.refs_2_, ...), custom_call_target="tpu_custom_call" | custom-call | tf_op jit(solution)/shard_map/outward/pallas_call | solution.py:564
